TPU v7x, 32 devices: a whole 2x2x4 slice. The times are simulated.
32 devices in a mesh: inner: 4 (over z), outer: 8 (over y, x, core).
Axes of the slice: x: 2, y: 2, z: 4, core: 2. Of those that a mesh axis runs over, the one named last changes fastest.
Arguments:
- features: bfloat16 [262144, 256], P(('inner', 'outer')), may hold values from -6 to 6
- tiles: bfloat16 [2048, 8, 128, 128], P(('inner', 'outer')), may hold values from -0.1875 to 0.1875
- tile_src: int32 [2048, 8], P(('inner', 'outer')), may hold values from 0 to 111, as said below
- tile_count: int32 [2048], P(('inner', 'outer')), may hold values from 1 to 8
- node_count: int32 [32], P(('inner', 'outer')), may hold values from 2730 to 8192
- boundary: int32 [32, 8], P(('inner', 'outer')), may hold values from 0 to 63, as said below
- send_inner: int32 [32, 4, 4], P(('inner', 'outer')), may hold values from 0 to 7
- count_inner: int32 [32, 4], P(('inner', 'outer')), may hold values from 0 to 4, as said below
- send_outer: int32 [32, 8, 4], P(('inner', 'outer')), may hold values from 0 to 7
- count_outer: int32 [32, 8], P(('inner', 'outer')), may hold values from 0 to 4, as said below
- w_first: bfloat16 [256, 256], replicated, may hold values from -0.375 to 0.375
- gamma: float32 [256], replicated, may hold values from 0.25 to 1.75
- beta: float32 [256], replicated, may hold values from -3 to 3
- w_second: bfloat16 [256, 256], replicated, may hold values from -0.375 to 0.375
- b_second: float32 [256], replicated, may hold values from -3 to 3
Outputs:
- updated: bfloat16 [262144, 256], P(('inner', 'outer'))
Inputs may be any that keep to these rules, and one draw needn't show every extreme that they name: `tile_src`: index into the partition's source table; a slot index that is read names a slot its sender fills. `boundary`: distinct block numbers within a partition. `count_inner`: zero toward the partition itself, at least one toward every other peer. `count_outer`: zero toward the partition itself, at least one toward every other peer.
All inputs are finite; a program needn't handle non-finite values.
Results may differ from a plain program's by a relative error of at most 0.0053.
Values may be sent and summed in bfloat16 or wider, within the bound.
A program may use at most 128 MiB of HBM per device.

v0:
```python
import math
import jax
import jax.numpy as jnp
from jax import lax
from jax.sharding import PartitionSpec as P

EPSILON = 1e-05


def packed(blocks, border, lists, counts, capacity):
    chosen = blocks[border[lists]]
    keep = jnp.arange(capacity)[None, :] < counts[:, None]
    return jnp.where(keep[:, :, None, None], chosen, jnp.zeros((), blocks.dtype))


def local(
    features,
    tiles,
    tile_src,
    tile_count,
    node_count,
    boundary,
    send_inner,
    count_inner,
    send_outer,
    count_outer,
    w_first,
    gamma,
    beta,
    w_second,
    b_second,
):
    node_dev, width = features.shape
    nblocks, per_block, block_rows = (tiles.shape[0], tiles.shape[1], tiles.shape[2])
    capacity = send_inner.shape[2]
    zero_bf = jnp.zeros((), jnp.bfloat16)
    filled = node_count[0]
    live = jnp.arange(node_dev) < filled
    features_live = jnp.where(live[:, None], features, zero_bf)
    blocks = features_live.reshape(nblocks, block_rows, width)
    border = boundary[0]
    from_inner = lax.all_to_all(
        packed(blocks, border, send_inner[0], count_inner[0], capacity),
        "inner",
        split_axis=0,
        concat_axis=0,
        tiled=True,
    )
    from_outer = lax.all_to_all(
        packed(blocks, border, send_outer[0], count_outer[0], capacity),
        "outer",
        split_axis=0,
        concat_axis=0,
        tiled=True,
    )
    table = jnp.concatenate(
        [
            blocks,
            from_inner.reshape(-1, block_rows, width),
            from_outer.reshape(-1, block_rows, width),
            jnp.zeros((1, block_rows, width), jnp.bfloat16),
        ],
        axis=0,
    )
    empty_slot = table.shape[0] - 1
    used = jnp.arange(per_block)[None, :] < tile_count[:, None]
    sources = jnp.where(used, tile_src, empty_slot)
    group = math.gcd(nblocks, 8)

    def aggregate(item):
        tile_group, source_group = item
        gathered = table[source_group]
        return jnp.einsum(
            "bjrk,bjkf->brf", tile_group, gathered, preferred_element_type=jnp.float32
        )

    summed = lax.map(
        aggregate,
        (
            tiles.reshape(-1, group, per_block, block_rows, block_rows),
            sources.reshape(-1, group, per_block),
        ),
    )
    combined = (features_live.astype(jnp.float32) + summed.reshape(node_dev, width)).astype(
        jnp.bfloat16
    )
    first = jnp.dot(combined, w_first, preferred_element_type=jnp.float32)
    count_local = filled.astype(jnp.float32).reshape(1)
    masked = jnp.where(live[:, None], first, 0.0)
    totals = lax.psum(
        (count_local, jnp.sum(masked, axis=0), jnp.sum(masked * masked, axis=0)), ("inner", "outer")
    )
    mean = totals[1] / totals[0]
    variance = totals[2] / totals[0] - mean * mean
    normed = jax.nn.relu(gamma * (first - mean) * lax.rsqrt(variance + EPSILON) + beta).astype(
        jnp.bfloat16
    )
    output = jnp.dot(normed, w_second, preferred_element_type=jnp.float32) + b_second
    return jnp.where(live[:, None], output, 0.0).astype(jnp.bfloat16)


def solution(mesh):
    in_specs = (
        P(("inner", "outer"), None),
        P(("inner", "outer"), None, None, None),
        P(("inner", "outer"), None),
        P(("inner", "outer")),
        P(("inner", "outer")),
        P(("inner", "outer"), None),
        P(("inner", "outer"), None, None),
        P(("inner", "outer"), None),
        P(("inner", "outer"), None, None),
        P(("inner", "outer"), None),
        P(),
        P(),
        P(),
        P(),
        P(),
    )
    out_specs = P(("inner", "outer"), None)
    return jax.shard_map(local, mesh=mesh, in_specs=in_specs, out_specs=out_specs, check_vma=False)
```

profile of v0, /device:TPU:12, one launch (start us, length us, event | category | flops | bytes accessed | tf_op | source)
XLA Modules:
  0.0 223.1 jit_solution(13318727625451619962)
XLA Ops:
  1.5 1.3 gather_fusion.1
  3.7 5.2 %broadcast_select_fusion = bf16[8192,256]{1,0:T(8,128)(2,1)} fusion(bf16[8192,256]{1,0:T(8,128)(2,1)} %param.17, pred[8192]{0:T(1024)(128)(4,1)S(1)} %iota_compare_fusion), kind=kLoop, calls=%fused_computation.27 | loop fusion | flops 2097152 | bytes 8396800 | tf_op jit(solution)/shard_map/jit(_where)/select_n | solution.py:39
  9.0 2.8 %gather_fusion.2 = bf16[16,128,256]{2,1,0:T(8,128)(2,1)S(1)} fusion(bf16[64,128,256]{2,1,0:T(8,128)(2,1)} %bitcast.65, s32[1024]{0:T(1024)S(1)} %pad_clamp_fusion.3), kind=kCustom, calls=%fused_computation.2 | custom fusion | bytes 2097216 | tf_op jit(solution)/shard_map/gather | solution.py:11
  11.8 1.1 broadcast_select_fusion.2
  12.9 5.3 %all-to-all-start = ((bf16[4,4,128,256]{3,2,1,0:T(8,128)(2,1)}), bf16[4,4,128,256]{3,2,1,0:T(8,128)(2,1)S(1)}, u32[]{:S(2)}, u32[]{:S(2)}) async-start(bf16[4,4,128,256]{3,2,1,0:T(8,128)(2,1)} %broadcast_select_fusion.2), calls=%async_computation | async-start | bytes 2097152 | tf_op jit(solution)/shard_map/all_to_all | solution.py:42
  19.5 2.9 %gather_fusion.4 = bf16[32,128,256]{2,1,0:T(8,128)(2,1)S(1)} fusion(bf16[64,128,256]{2,1,0:T(8,128)(2,1)} %bitcast.66, s32[1024]{0:T(1024)S(1)} %pad_clamp_fusion.1), kind=kCustom, calls=%fused_computation.4 | custom fusion | bytes 4194432 | tf_op jit(solution)/shard_map/gather | solution.py:11
  22.4 1.6 broadcast_select_fusion.1
  24.0 16.6 %all-to-all-done = bf16[4,4,128,256]{3,2,1,0:T(8,128)(2,1)S(1)} async-done(((bf16[4,4,128,256]{3,2,1,0:T(8,128)(2,1)}), bf16[4,4,128,256]{3,2,1,0:T(8,128)(2,1)S(1)}, u32[]{:S(2)}, u32[]{:S(2)}) %all-to-all-start) | async-done | bytes 1048608 | tf_op jit(solution)/shard_map/all_to_all | solution.py:42
  40.7 4.2 %all-to-all-start.1 = ((bf16[8,4,128,256]{3,2,1,0:T(8,128)(2,1)}), bf16[8,4,128,256]{3,2,1,0:T(8,128)(2,1)S(1)}, u32[]{:S(2)}, u32[]{:S(2)}) async-start(bf16[8,4,128,256]{3,2,1,0:T(8,128)(2,1)} %broadcast_select_fusion.1), calls=%async_computation.1 | async-start | bytes 4194304 | tf_op jit(solution)/shard_map/all_to_all | solution.py:49
  45.1 25.0 %all-to-all-done.1 = bf16[8,4,128,256]{3,2,1,0:T(8,128)(2,1)S(1)} async-done(((bf16[8,4,128,256]{3,2,1,0:T(8,128)(2,1)}), bf16[8,4,128,256]{3,2,1,0:T(8,128)(2,1)S(1)}, u32[]{:S(2)}, u32[]{:S(2)}) %all-to-all-start.1) | async-done | bytes 2097184 | tf_op jit(solution)/shard_map/all_to_all | solution.py:49
  70.1 6.0 %maximum_maximum_fusion = bf16[113,128,256]{2,1,0:T(8,128)(2,1)} fusion(bf16[32,128,256]{2,1,0:T(8,128)(2,1)S(1)} %bitcast.69, bf16[16,128,256]{2,1,0:T(8,128)(2,1)S(1)} %bitcast.71, bf16[64,128,256]{2,1,0:T(8,128)(2,1)} %bitcast.67, bf16[113]{0:T(256)(128)(2,1)S(1)} %pad.3.clone), kind=kLoop, calls=%fused_computation.21 | loop fusion | flops 11108352 | bytes 14745826 | tf_op jit(solution)/shard_map/concatenate | solution.py:56
  76.1 85.3 %while.10 = (s32[]{:T(128)}, f32[8,8,128,256]{3,2,1,0:T(8,128)}, bf16[8,8,8,128,128]{4,3,2,1,0:T(8,128)(2,1)}, s32[8,8,8]{2,1,0:T(8,128)S(1)}, bf16[113,128,256]{2,1,0:T(8,128)(2,1)}, /*index=5*/s32[]{:T(128)}) while((s32[]{:T(128)}, f32[8,8,128,256]{3,2,1,0:T(8,128)}, bf16[8,8,8,128,128]{4,3,2,1,0:T(8,128)(2,1)}, s32[8,8,8]{2,1,0:T(8,128)S(1)}, ...), condition=%wide.region_1.2_spmd, body=%wide.region_0.1_spmd.sunk | while | flops 536872128 | bytes 15735369 | solution.py:77
  76.2 5.9 %gather_fusion = bf16[64,128,256]{2,1,0:T(8,128)(2,1)} fusion(bf16[113,128,256]{2,1,0:T(8,128)(2,1)} %get-tuple-element.98, s32[1024]{0:T(1024)S(1)} %pad_clamp_fusion.6), kind=kCustom, calls=%fused_computation.clone.1 | custom fusion | bytes 8388864 | tf_op jit(solution)/shard_map/while/body/eval_jaxpr/gather | solution.py:72
  82.1 4.6 %fusion.29 = f32[8,8,128,256]{3,2,1,0:T(8,128)} fusion(f32[8,8,128,256]{3,2,1,0:T(8,128)} %get-tuple-element.89, s32[]{:T(128)} %get-tuple-element.88, bf16[8,8,128,256]{3,2,1,0:T(8,128)(2,1)} %bitcast.64, bf16[8,8,8,128,128]{4,3,2,1,0:T(8,128)(2,1)} %get-tuple-element.96), kind=kOutput, calls=%fused_computation.9.clone.1 | convolution fusion | flops 536870912 | bytes 7341056 | tf_op jit(solution)/shard_map/while/body/eval_jaxpr/bjrk,bjkf->brf/dot_general | solution.py:73
  86.8 5.9 %gather_fusion = bf16[64,128,256]{2,1,0:T(8,128)(2,1)} fusion(bf16[113,128,256]{2,1,0:T(8,128)(2,1)} %get-tuple-element.98, s32[1024]{0:T(1024)S(1)} %pad_clamp_fusion.6), kind=kCustom, calls=%fused_computation.clone.1 | custom fusion | bytes 8388864 | tf_op jit(solution)/shard_map/while/body/eval_jaxpr/gather | solution.py:72
  92.8 4.7 %fusion.29 = f32[8,8,128,256]{3,2,1,0:T(8,128)} fusion(f32[8,8,128,256]{3,2,1,0:T(8,128)} %get-tuple-element.89, s32[]{:T(128)} %get-tuple-element.88, bf16[8,8,128,256]{3,2,1,0:T(8,128)(2,1)} %bitcast.64, bf16[8,8,8,128,128]{4,3,2,1,0:T(8,128)(2,1)} %get-tuple-element.96), kind=kOutput, calls=%fused_computation.9.clone.1 | convolution fusion | flops 536870912 | bytes 7341056 | tf_op jit(solution)/shard_map/while/body/eval_jaxpr/bjrk,bjkf->brf/dot_general | solution.py:73
  97.5 5.9 %gather_fusion = bf16[64,128,256]{2,1,0:T(8,128)(2,1)} fusion(bf16[113,128,256]{2,1,0:T(8,128)(2,1)} %get-tuple-element.98, s32[1024]{0:T(1024)S(1)} %pad_clamp_fusion.6), kind=kCustom, calls=%fused_computation.clone.1 | custom fusion | bytes 8388864 | tf_op jit(solution)/shard_map/while/body/eval_jaxpr/gather | solution.py:72
  103.5 4.6 %fusion.29 = f32[8,8,128,256]{3,2,1,0:T(8,128)} fusion(f32[8,8,128,256]{3,2,1,0:T(8,128)} %get-tuple-element.89, s32[]{:T(128)} %get-tuple-element.88, bf16[8,8,128,256]{3,2,1,0:T(8,128)(2,1)} %bitcast.64, bf16[8,8,8,128,128]{4,3,2,1,0:T(8,128)(2,1)} %get-tuple-element.96), kind=kOutput, calls=%fused_computation.9.clone.1 | convolution fusion | flops 536870912 | bytes 7341056 | tf_op jit(solution)/shard_map/while/body/eval_jaxpr/bjrk,bjkf->brf/dot_general | solution.py:73
  108.2 5.9 %gather_fusion = bf16[64,128,256]{2,1,0:T(8,128)(2,1)} fusion(bf16[113,128,256]{2,1,0:T(8,128)(2,1)} %get-tuple-element.98, s32[1024]{0:T(1024)S(1)} %pad_clamp_fusion.6), kind=kCustom, calls=%fused_computation.clone.1 | custom fusion | bytes 8388864 | tf_op jit(solution)/shard_map/while/body/eval_jaxpr/gather | solution.py:72
  114.1 4.6 %fusion.29 = f32[8,8,128,256]{3,2,1,0:T(8,128)} fusion(f32[8,8,128,256]{3,2,1,0:T(8,128)} %get-tuple-element.89, s32[]{:T(128)} %get-tuple-element.88, bf16[8,8,128,256]{3,2,1,0:T(8,128)(2,1)} %bitcast.64, bf16[8,8,8,128,128]{4,3,2,1,0:T(8,128)(2,1)} %get-tuple-element.96), kind=kOutput, calls=%fused_computation.9.clone.1 | convolution fusion | flops 536870912 | bytes 7341056 | tf_op jit(solution)/shard_map/while/body/eval_jaxpr/bjrk,bjkf->brf/dot_general | solution.py:73
  118.9 5.9 %gather_fusion = bf16[64,128,256]{2,1,0:T(8,128)(2,1)} fusion(bf16[113,128,256]{2,1,0:T(8,128)(2,1)} %get-tuple-element.98, s32[1024]{0:T(1024)S(1)} %pad_clamp_fusion.6), kind=kCustom, calls=%fused_computation.clone.1 | custom fusion | bytes 8388864 | tf_op jit(solution)/shard_map/while/body/eval_jaxpr/gather | solution.py:72
  124.8 4.6 %fusion.29 = f32[8,8,128,256]{3,2,1,0:T(8,128)} fusion(f32[8,8,128,256]{3,2,1,0:T(8,128)} %get-tuple-element.89, s32[]{:T(128)} %get-tuple-element.88, bf16[8,8,128,256]{3,2,1,0:T(8,128)(2,1)} %bitcast.64, bf16[8,8,8,128,128]{4,3,2,1,0:T(8,128)(2,1)} %get-tuple-element.96), kind=kOutput, calls=%fused_computation.9.clone.1 | convolution fusion | flops 536870912 | bytes 7341056 | tf_op jit(solution)/shard_map/while/body/eval_jaxpr/bjrk,bjkf->brf/dot_general | solution.py:73
  129.5 5.9 %gather_fusion = bf16[64,128,256]{2,1,0:T(8,128)(2,1)} fusion(bf16[113,128,256]{2,1,0:T(8,128)(2,1)} %get-tuple-element.98, s32[1024]{0:T(1024)S(1)} %pad_clamp_fusion.6), kind=kCustom, calls=%fused_computation.clone.1 | custom fusion | bytes 8388864 | tf_op jit(solution)/shard_map/while/body/eval_jaxpr/gather | solution.py:72
  135.4 4.6 %fusion.29 = f32[8,8,128,256]{3,2,1,0:T(8,128)} fusion(f32[8,8,128,256]{3,2,1,0:T(8,128)} %get-tuple-element.89, s32[]{:T(128)} %get-tuple-element.88, bf16[8,8,128,256]{3,2,1,0:T(8,128)(2,1)} %bitcast.64, bf16[8,8,8,128,128]{4,3,2,1,0:T(8,128)(2,1)} %get-tuple-element.96), kind=kOutput, calls=%fused_computation.9.clone.1 | convolution fusion | flops 536870912 | bytes 7341056 | tf_op jit(solution)/shard_map/while/body/eval_jaxpr/bjrk,bjkf->brf/dot_general | solution.py:73
  140.2 5.9 %gather_fusion = bf16[64,128,256]{2,1,0:T(8,128)(2,1)} fusion(bf16[113,128,256]{2,1,0:T(8,128)(2,1)} %get-tuple-element.98, s32[1024]{0:T(1024)S(1)} %pad_clamp_fusion.6), kind=kCustom, calls=%fused_computation.clone.1 | custom fusion | bytes 8388864 | tf_op jit(solution)/shard_map/while/body/eval_jaxpr/gather | solution.py:72
  146.1 4.6 %fusion.29 = f32[8,8,128,256]{3,2,1,0:T(8,128)} fusion(f32[8,8,128,256]{3,2,1,0:T(8,128)} %get-tuple-element.89, s32[]{:T(128)} %get-tuple-element.88, bf16[8,8,128,256]{3,2,1,0:T(8,128)(2,1)} %bitcast.64, bf16[8,8,8,128,128]{4,3,2,1,0:T(8,128)(2,1)} %get-tuple-element.96), kind=kOutput, calls=%fused_computation.9.clone.1 | convolution fusion | flops 536870912 | bytes 7341056 | tf_op jit(solution)/shard_map/while/body/eval_jaxpr/bjrk,bjkf->brf/dot_general | solution.py:73
  150.8 5.9 %gather_fusion = bf16[64,128,256]{2,1,0:T(8,128)(2,1)} fusion(bf16[113,128,256]{2,1,0:T(8,128)(2,1)} %get-tuple-element.98, s32[1024]{0:T(1024)S(1)} %pad_clamp_fusion.6), kind=kCustom, calls=%fused_computation.clone.1 | custom fusion | bytes 8388864 | tf_op jit(solution)/shard_map/while/body/eval_jaxpr/gather | solution.py:72
  156.8 4.7 %fusion.29 = f32[8,8,128,256]{3,2,1,0:T(8,128)} fusion(f32[8,8,128,256]{3,2,1,0:T(8,128)} %get-tuple-element.89, s32[]{:T(128)} %get-tuple-element.88, bf16[8,8,128,256]{3,2,1,0:T(8,128)(2,1)} %bitcast.64, bf16[8,8,8,128,128]{4,3,2,1,0:T(8,128)(2,1)} %get-tuple-element.96), kind=kOutput, calls=%fused_computation.9.clone.1 | convolution fusion | flops 536870912 | bytes 7341056 | tf_op jit(solution)/shard_map/while/body/eval_jaxpr/bjrk,bjkf->brf/dot_general | solution.py:73
  161.4 5.5 %fusion.12 = bf16[8192,256]{1,0:T(8,128)(2,1)S(1)} fusion(f32[8,8,128,256]{3,2,1,0:T(8,128)} %get-tuple-element.32, bf16[8192,256]{1,0:T(8,128)(2,1)} %param.17, pred[8192]{0:T(1024)(128)(4,1)S(1)} %iota_compare_fusion), kind=kLoop, calls=%fused_computation.17 | loop fusion | flops 8388608 | bytes 16785408 | tf_op jit(solution)/shard_map/convert_element_type | solution.py:84
  167.0 6.5 %multiply_reduce_fusion = (f32[256]{0:T(256)S(1)}, f32[256]{0:T(256)S(1)}, f32[8192,256]{1,0:T(8,128)}) fusion(pred[8192]{0:T(1024)(128)(4,1)S(1)} %iota_compare_fusion, bf16[8192,256]{1,0:T(8,128)(2,1)S(1)} %fusion.12, bf16[256,256]{1,0:T(8,128)(2,1)S(1)} %copy-done), kind=kOutput, calls=%fused_computation.19 | convolution fusion | flops 1082129920 | bytes 12724224 | tf_op jit(solution)/shard_map/dot_general | solution.py:87
  173.5 42.9 %all-reduce = (f32[256]{0:T(256)S(1)}, f32[]{:T(128)}, f32[256]{0:T(256)S(1)}) all-reduce(f32[256]{0:T(256)S(1)} %get-tuple-element.34, f32[]{:T(128)S(6)} %convert_element_type.17, f32[256]{0:T(256)S(1)} %get-tuple-element.33), channel_id=1, replica_groups=mesh['inner'=4,'outer'=8] {'inner','outer'}, use_global_device_ids=true, to_apply=%region_3.4 | all-reduce | flops 513 | bytes 4104 | tf_op jit(solution)/shard_map/psum | solution.py:90
  217.0 6.1 %fusion.11 = bf16[8192,256]{1,0:T(8,128)(2,1)} fusion(bf16[256,256]{1,0:T(8,128)(2,1)S(1)} %copy-done.5, f32[8192,256]{1,0:T(8,128)} %get-tuple-element.50, f32[256]{0:T(256)S(1)} %copy-done.6, f32[256]{0:T(256)S(1)} %copy-done.7, f32[256]{0:T(256)S(1)} %get-tuple-element.48, f32[256]{0:T(256)S(1)} %get-tuple-element.49, f32[256]{0:T(256)S(1)} %copy-done.8, ...), kind=kOutput, calls=%fused_computation.15 | convolution fusion | flops 1092616192 | bytes 12727296 | tf_op jit(solution)/shard_map/dot_general | solution.py:98
  (70 shorter events, 4.6 us)
Async XLA Ops:
  0.0 167.0 %copy-start = (bf16[256,256]{1,0:T(8,128)(2,1)S(1)}, bf16[256,256]{1,0:T(8,128)(2,1)}, u32[]{:S(2)}) copy-start(bf16[256,256]{1,0:T(8,128)(2,1)} %param.27) | copy-start | bytes 393220
  2.8 15.4 %copy-start.3 = (s32[1,8,4]{1,2,0:T(4,128)S(1)}, s32[1,8,4]{1,2,0:T(4,128)}, u32[]{:S(2)}) copy-start(s32[1,8,4]{1,2,0:T(4,128)} %param.25) | copy-start | bytes 388
  2.8 15.6 %copy-start.1 = (s32[1,8]{1,0:T(1,128)S(1)}, s32[1,8]{1,0:T(1,128)}, u32[]{:S(2)}) copy-start(s32[1,8]{1,0:T(1,128)} %param.22) | copy-start | bytes 100
  9.0 13.4 %copy-start.9 = (s32[1,8]{1,0:T(1,128)S(1)}, s32[1,8]{1,0:T(1,128)}, u32[]{:S(2)}) copy-start(s32[1,8]{1,0:T(1,128)} %param.26) | copy-start | bytes 100
  12.9 27.8 %all-to-all-start = ((bf16[4,4,128,256]{3,2,1,0:T(8,128)(2,1)}), bf16[4,4,128,256]{3,2,1,0:T(8,128)(2,1)S(1)}, u32[]{:S(2)}, u32[]{:S(2)}) async-start(bf16[4,4,128,256]{3,2,1,0:T(8,128)(2,1)} %broadcast_select_fusion.2), calls=%async_computation | async-start | bytes 2097152 | tf_op jit(solution)/shard_map/all_to_all | solution.py:42
  18.4 26.5 %copy-start.2 = (s32[64,8]{0,1:T(8,128)S(1)}, s32[64,8]{0,1:T(8,128)}, u32[]{:S(2)}) copy-start(s32[64,8]{0,1:T(8,128)} %param.19) | copy-start | bytes 6148
  18.4 26.5 %copy-start.4 = (s32[64]{0:T(128)S(1)}, s32[64]{0:T(128)}, u32[]{:S(2)}) copy-start(s32[64]{0:T(128)} %param.20) | copy-start | bytes 772
  40.7 29.4 %all-to-all-start.1 = ((bf16[8,4,128,256]{3,2,1,0:T(8,128)(2,1)}), bf16[8,4,128,256]{3,2,1,0:T(8,128)(2,1)S(1)}, u32[]{:S(2)}, u32[]{:S(2)}) async-start(bf16[8,4,128,256]{3,2,1,0:T(8,128)(2,1)} %broadcast_select_fusion.1), calls=%async_computation.1 | async-start | bytes 4194304 | tf_op jit(solution)/shard_map/all_to_all | solution.py:49
  167.0 50.0 %copy-start.5 = (bf16[256,256]{1,0:T(8,128)(2,1)S(1)}, bf16[256,256]{1,0:T(8,128)(2,1)}, u32[]{:S(2)}) copy-start(bf16[256,256]{1,0:T(8,128)(2,1)} %param.30) | copy-start | bytes 393220
  167.0 50.0 %copy-start.6 = (f32[256]{0:T(256)S(1)}, f32[256]{0:T(256)}, u32[]{:S(2)}) copy-start(f32[256]{0:T(256)} %param.31) | copy-start | bytes 3076
  167.0 50.0 %copy-start.7 = (f32[256]{0:T(256)S(1)}, f32[256]{0:T(256)}, u32[]{:S(2)}) copy-start(f32[256]{0:T(256)} %param.29) | copy-start | bytes 3076
  167.0 50.0 %copy-start.8 = (f32[256]{0:T(256)S(1)}, f32[256]{0:T(256)}, u32[]{:S(2)}) copy-start(f32[256]{0:T(256)} %param.28) | copy-start | bytes 3076
where the time goes:
time: 224 us; the launch traced here: 223 us
  local copies, waits for them, and re-layouts  56.8 us (25%)
  matrix products  49.6 us (22%)
  blocking collectives  42.9 us (19%)
  waiting for transfers between devices  41.6 us (19%)
  other arithmetic  21.8 us (10%)
  starting transfers between devices  9.54 us (4%)
    gather x8, local copies, waits for them, and re-layouts, aggregate(): gathered = table[source_group]  47.4 us
    psum x1, blocking collectives, local(): lax.psum((count_local, jnp.sum(masked, axis=0), jnp.sum(masked * masked,...  42.9 us
    dot_general x8, matrix products, aggregate(): jnp.einsum('bjrk,bjkf->brf', tile_group, gathered, preferred_element_type...  37.1 us
    all_to_all x1, waiting for transfers between devices, local(): lax.all_to_all(packed(blocks, border, send_outer[0], count_outer[0], capa...  25 us
    all_to_all x1, waiting for transfers between devices, local(): lax.all_to_all(packed(blocks, border, send_inner[0], count_inner[0], capa...  16.6 us
    gather x7, local copies, waits for them, and re-layouts, packed(): chosen = blocks[border[lists]]  7.94 us
    dot_general x1, matrix products, local(): first = jnp.dot(combined, w_first, preferred_element_type=jnp.float32)  6.45 us
    dot_general x1, matrix products, local(): jnp.dot(normed, w_second, preferred_element_type=jnp.float32) + b_second  6.09 us
  transfers between devices with their start and end apart: 2, of which 2 were waited for; matrix products, arithmetic and copies ran while one was open for 3% of the time, Pallas kernels for 0%

commit v1 on v0

--- a/solution.py
+++ b/solution.py
@@ -87,9 +87,9 @@
     first = jnp.dot(combined, w_first, preferred_element_type=jnp.float32)
     count_local = filled.astype(jnp.float32).reshape(1)
     masked = jnp.where(live[:, None], first, 0.0)
-    totals = lax.psum(
-        (count_local, jnp.sum(masked, axis=0), jnp.sum(masked * masked, axis=0)), ("inner", "outer")
-    )
+    totals = (count_local, jnp.sum(masked, axis=0), jnp.sum(masked * masked, axis=0))
+    for jj in ("outer", "inner"):
+        totals = jax.lax.psum(totals, jj)
     mean = totals[1] / totals[0]
     variance = totals[2] / totals[0] - mean * mean
     normed = jax.nn.relu(gamma * (first - mean) * lax.rsqrt(variance + EPSILON) + beta).astype(

time: 224 us -> 210 us (0.938); the launches traced: 223 us -> 206 us
  blocking collectives: 42.9 us -> 26.2 us
    psum x1 -> x2, blocking collectives: 42.9 us -> 26.2 us  [local(): totals = jax.lax.psum(totals, jj)]
where the time goes in v1:
time: 210 us; the launch traced here: 206 us
  local copies, waits for them, and re-layouts  56.8 us (27%)
  matrix products  49.7 us (24%)
  waiting for transfers between devices  41.6 us (20%)
  blocking collectives  26.2 us (12%)
  other arithmetic  21.7 us (10%)
  starting transfers between devices  9.54 us (5%)
    gather x8, local copies, waits for them, and re-layouts, aggregate(): gathered = table[source_group]  47.4 us
    dot_general x8, matrix products, aggregate(): jnp.einsum('bjrk,bjkf->brf', tile_group, gathered, preferred_element_type...  37.1 us
    psum x2, blocking collectives, local(): totals = jax.lax.psum(totals, jj)  26.2 us
    all_to_all x1, waiting for transfers between devices, local(): lax.all_to_all(packed(blocks, border, send_outer[0], count_outer[0], capa...  25 us
    all_to_all x1, waiting for transfers between devices, local(): lax.all_to_all(packed(blocks, border, send_inner[0], count_inner[0], capa...  16.7 us
    gather x7, local copies, waits for them, and re-layouts, packed(): chosen = blocks[border[lists]]  7.94 us
    dot_general x1, matrix products, local(): first = jnp.dot(combined, w_first, preferred_element_type=jnp.float32)  6.44 us
    dot_general x1, matrix products, local(): jnp.dot(normed, w_second, preferred_element_type=jnp.float32) + b_second  6.09 us
  transfers between devices with their start and end apart: 2, of which 2 were waited for; matrix products, arithmetic and copies ran while one was open for 3% of the time, Pallas kernels for 0%

profile of v1, /device:TPU:12, one launch (start us, length us, event | category | flops | bytes accessed | tf_op | source)
XLA Modules:
  0.0 206.4 jit_solution(1146683624874542538)
XLA Ops:
  1.5 1.3 gather_fusion.1
  3.7 5.2 %broadcast_select_fusion = bf16[8192,256]{1,0:T(8,128)(2,1)} fusion(bf16[8192,256]{1,0:T(8,128)(2,1)} %param.17, pred[8192]{0:T(1024)(128)(4,1)S(1)} %iota_compare_fusion), kind=kLoop, calls=%fused_computation.27 | loop fusion | flops 2097152 | bytes 8396800 | tf_op jit(solution)/shard_map/jit(_where)/select_n | solution.py:39
  9.0 2.8 %gather_fusion.2 = bf16[16,128,256]{2,1,0:T(8,128)(2,1)S(1)} fusion(bf16[64,128,256]{2,1,0:T(8,128)(2,1)} %bitcast.67, s32[1024]{0:T(1024)S(1)} %pad_clamp_fusion.3), kind=kCustom, calls=%fused_computation.2 | custom fusion | bytes 2097216 | tf_op jit(solution)/shard_map/gather | solution.py:11
  12.9 5.3 %all-to-all-start = ((bf16[4,4,128,256]{3,2,1,0:T(8,128)(2,1)}), bf16[4,4,128,256]{3,2,1,0:T(8,128)(2,1)S(1)}, u32[]{:S(2)}, u32[]{:S(2)}) async-start(bf16[4,4,128,256]{3,2,1,0:T(8,128)(2,1)} %broadcast_select_fusion.2), calls=%async_computation | async-start | bytes 2097152 | tf_op jit(solution)/shard_map/all_to_all | solution.py:42
  19.5 2.9 %gather_fusion.4 = bf16[32,128,256]{2,1,0:T(8,128)(2,1)S(1)} fusion(bf16[64,128,256]{2,1,0:T(8,128)(2,1)} %bitcast.68, s32[1024]{0:T(1024)S(1)} %pad_clamp_fusion.1), kind=kCustom, calls=%fused_computation.4 | custom fusion | bytes 4194432 | tf_op jit(solution)/shard_map/gather | solution.py:11
  22.5 1.6 broadcast_select_fusion.1
  24.0 16.7 %all-to-all-done = bf16[4,4,128,256]{3,2,1,0:T(8,128)(2,1)S(1)} async-done(((bf16[4,4,128,256]{3,2,1,0:T(8,128)(2,1)}), bf16[4,4,128,256]{3,2,1,0:T(8,128)(2,1)S(1)}, u32[]{:S(2)}, u32[]{:S(2)}) %all-to-all-start) | async-done | bytes 1048608 | tf_op jit(solution)/shard_map/all_to_all | solution.py:42
  40.7 4.2 %all-to-all-start.1 = ((bf16[8,4,128,256]{3,2,1,0:T(8,128)(2,1)}), bf16[8,4,128,256]{3,2,1,0:T(8,128)(2,1)S(1)}, u32[]{:S(2)}, u32[]{:S(2)}) async-start(bf16[8,4,128,256]{3,2,1,0:T(8,128)(2,1)} %broadcast_select_fusion.1), calls=%async_computation.1 | async-start | bytes 4194304 | tf_op jit(solution)/shard_map/all_to_all | solution.py:49
  45.1 25.0 %all-to-all-done.1 = bf16[8,4,128,256]{3,2,1,0:T(8,128)(2,1)S(1)} async-done(((bf16[8,4,128,256]{3,2,1,0:T(8,128)(2,1)}), bf16[8,4,128,256]{3,2,1,0:T(8,128)(2,1)S(1)}, u32[]{:S(2)}, u32[]{:S(2)}) %all-to-all-start.1) | async-done | bytes 2097184 | tf_op jit(solution)/shard_map/all_to_all | solution.py:49
  70.1 6.0 %maximum_maximum_fusion = bf16[113,128,256]{2,1,0:T(8,128)(2,1)} fusion(bf16[32,128,256]{2,1,0:T(8,128)(2,1)S(1)} %bitcast.71, bf16[16,128,256]{2,1,0:T(8,128)(2,1)S(1)} %bitcast.73, bf16[64,128,256]{2,1,0:T(8,128)(2,1)} %bitcast.69, bf16[113]{0:T(256)(128)(2,1)S(1)} %pad.3.clone), kind=kLoop, calls=%fused_computation.21 | loop fusion | flops 11108352 | bytes 14745826 | tf_op jit(solution)/shard_map/concatenate | solution.py:56
  76.0 85.3 %while.10 = (s32[]{:T(128)}, f32[8,8,128,256]{3,2,1,0:T(8,128)}, bf16[8,8,8,128,128]{4,3,2,1,0:T(8,128)(2,1)}, s32[8,8,8]{2,1,0:T(8,128)S(1)}, bf16[113,128,256]{2,1,0:T(8,128)(2,1)}, /*index=5*/s32[]{:T(128)}) while((s32[]{:T(128)}, f32[8,8,128,256]{3,2,1,0:T(8,128)}, bf16[8,8,8,128,128]{4,3,2,1,0:T(8,128)(2,1)}, s32[8,8,8]{2,1,0:T(8,128)S(1)}, ...), condition=%wide.region_1.2_spmd, body=%wide.region_0.1_spmd.sunk | while | flops 536872128 | bytes 15735369 | solution.py:77
  76.1 5.9 %gather_fusion = bf16[64,128,256]{2,1,0:T(8,128)(2,1)} fusion(bf16[113,128,256]{2,1,0:T(8,128)(2,1)} %get-tuple-element.101, s32[1024]{0:T(1024)S(1)} %pad_clamp_fusion.6), kind=kCustom, calls=%fused_computation.clone.1 | custom fusion | bytes 8388864 | tf_op jit(solution)/shard_map/while/body/eval_jaxpr/gather | solution.py:72
  82.1 4.6 %fusion.29 = f32[8,8,128,256]{3,2,1,0:T(8,128)} fusion(f32[8,8,128,256]{3,2,1,0:T(8,128)} %get-tuple-element.92, s32[]{:T(128)} %get-tuple-element.91, bf16[8,8,128,256]{3,2,1,0:T(8,128)(2,1)} %bitcast.66, bf16[8,8,8,128,128]{4,3,2,1,0:T(8,128)(2,1)} %get-tuple-element.99), kind=kOutput, calls=%fused_computation.9.clone.1 | convolution fusion | flops 536870912 | bytes 7341056 | tf_op jit(solution)/shard_map/while/body/eval_jaxpr/bjrk,bjkf->brf/dot_general | solution.py:73
  86.8 5.9 %gather_fusion = bf16[64,128,256]{2,1,0:T(8,128)(2,1)} fusion(bf16[113,128,256]{2,1,0:T(8,128)(2,1)} %get-tuple-element.101, s32[1024]{0:T(1024)S(1)} %pad_clamp_fusion.6), kind=kCustom, calls=%fused_computation.clone.1 | custom fusion | bytes 8388864 | tf_op jit(solution)/shard_map/while/body/eval_jaxpr/gather | solution.py:72
  92.7 4.7 %fusion.29 = f32[8,8,128,256]{3,2,1,0:T(8,128)} fusion(f32[8,8,128,256]{3,2,1,0:T(8,128)} %get-tuple-element.92, s32[]{:T(128)} %get-tuple-element.91, bf16[8,8,128,256]{3,2,1,0:T(8,128)(2,1)} %bitcast.66, bf16[8,8,8,128,128]{4,3,2,1,0:T(8,128)(2,1)} %get-tuple-element.99), kind=kOutput, calls=%fused_computation.9.clone.1 | convolution fusion | flops 536870912 | bytes 7341056 | tf_op jit(solution)/shard_map/while/body/eval_jaxpr/bjrk,bjkf->brf/dot_general | solution.py:73
  97.5 5.9 %gather_fusion = bf16[64,128,256]{2,1,0:T(8,128)(2,1)} fusion(bf16[113,128,256]{2,1,0:T(8,128)(2,1)} %get-tuple-element.101, s32[1024]{0:T(1024)S(1)} %pad_clamp_fusion.6), kind=kCustom, calls=%fused_computation.clone.1 | custom fusion | bytes 8388864 | tf_op jit(solution)/shard_map/while/body/eval_jaxpr/gather | solution.py:72
  103.4 4.6 %fusion.29 = f32[8,8,128,256]{3,2,1,0:T(8,128)} fusion(f32[8,8,128,256]{3,2,1,0:T(8,128)} %get-tuple-element.92, s32[]{:T(128)} %get-tuple-element.91, bf16[8,8,128,256]{3,2,1,0:T(8,128)(2,1)} %bitcast.66, bf16[8,8,8,128,128]{4,3,2,1,0:T(8,128)(2,1)} %get-tuple-element.99), kind=kOutput, calls=%fused_computation.9.clone.1 | convolution fusion | flops 536870912 | bytes 7341056 | tf_op jit(solution)/shard_map/while/body/eval_jaxpr/bjrk,bjkf->brf/dot_general | solution.py:73
  108.1 5.9 %gather_fusion = bf16[64,128,256]{2,1,0:T(8,128)(2,1)} fusion(bf16[113,128,256]{2,1,0:T(8,128)(2,1)} %get-tuple-element.101, s32[1024]{0:T(1024)S(1)} %pad_clamp_fusion.6), kind=kCustom, calls=%fused_computation.clone.1 | custom fusion | bytes 8388864 | tf_op jit(solution)/shard_map/while/body/eval_jaxpr/gather | solution.py:72
  114.1 4.6 %fusion.29 = f32[8,8,128,256]{3,2,1,0:T(8,128)} fusion(f32[8,8,128,256]{3,2,1,0:T(8,128)} %get-tuple-element.92, s32[]{:T(128)} %get-tuple-element.91, bf16[8,8,128,256]{3,2,1,0:T(8,128)(2,1)} %bitcast.66, bf16[8,8,8,128,128]{4,3,2,1,0:T(8,128)(2,1)} %get-tuple-element.99), kind=kOutput, calls=%fused_computation.9.clone.1 | convolution fusion | flops 536870912 | bytes 7341056 | tf_op jit(solution)/shard_map/while/body/eval_jaxpr/bjrk,bjkf->brf/dot_general | solution.py:73
  118.8 5.9 %gather_fusion = bf16[64,128,256]{2,1,0:T(8,128)(2,1)} fusion(bf16[113,128,256]{2,1,0:T(8,128)(2,1)} %get-tuple-element.101, s32[1024]{0:T(1024)S(1)} %pad_clamp_fusion.6), kind=kCustom, calls=%fused_computation.clone.1 | custom fusion | bytes 8388864 | tf_op jit(solution)/shard_map/while/body/eval_jaxpr/gather | solution.py:72
  124.7 4.6 %fusion.29 = f32[8,8,128,256]{3,2,1,0:T(8,128)} fusion(f32[8,8,128,256]{3,2,1,0:T(8,128)} %get-tuple-element.92, s32[]{:T(128)} %get-tuple-element.91, bf16[8,8,128,256]{3,2,1,0:T(8,128)(2,1)} %bitcast.66, bf16[8,8,8,128,128]{4,3,2,1,0:T(8,128)(2,1)} %get-tuple-element.99), kind=kOutput, calls=%fused_computation.9.clone.1 | convolution fusion | flops 536870912 | bytes 7341056 | tf_op jit(solution)/shard_map/while/body/eval_jaxpr/bjrk,bjkf->brf/dot_general | solution.py:73
  129.4 5.9 %gather_fusion = bf16[64,128,256]{2,1,0:T(8,128)(2,1)} fusion(bf16[113,128,256]{2,1,0:T(8,128)(2,1)} %get-tuple-element.101, s32[1024]{0:T(1024)S(1)} %pad_clamp_fusion.6), kind=kCustom, calls=%fused_computation.clone.1 | custom fusion | bytes 8388864 | tf_op jit(solution)/shard_map/while/body/eval_jaxpr/gather | solution.py:72
  135.4 4.7 %fusion.29 = f32[8,8,128,256]{3,2,1,0:T(8,128)} fusion(f32[8,8,128,256]{3,2,1,0:T(8,128)} %get-tuple-element.92, s32[]{:T(128)} %get-tuple-element.91, bf16[8,8,128,256]{3,2,1,0:T(8,128)(2,1)} %bitcast.66, bf16[8,8,8,128,128]{4,3,2,1,0:T(8,128)(2,1)} %get-tuple-element.99), kind=kOutput, calls=%fused_computation.9.clone.1 | convolution fusion | flops 536870912 | bytes 7341056 | tf_op jit(solution)/shard_map/while/body/eval_jaxpr/bjrk,bjkf->brf/dot_general | solution.py:73
  140.1 5.9 %gather_fusion = bf16[64,128,256]{2,1,0:T(8,128)(2,1)} fusion(bf16[113,128,256]{2,1,0:T(8,128)(2,1)} %get-tuple-element.101, s32[1024]{0:T(1024)S(1)} %pad_clamp_fusion.6), kind=kCustom, calls=%fused_computation.clone.1 | custom fusion | bytes 8388864 | tf_op jit(solution)/shard_map/while/body/eval_jaxpr/gather | solution.py:72
  146.1 4.6 %fusion.29 = f32[8,8,128,256]{3,2,1,0:T(8,128)} fusion(f32[8,8,128,256]{3,2,1,0:T(8,128)} %get-tuple-element.92, s32[]{:T(128)} %get-tuple-element.91, bf16[8,8,128,256]{3,2,1,0:T(8,128)(2,1)} %bitcast.66, bf16[8,8,8,128,128]{4,3,2,1,0:T(8,128)(2,1)} %get-tuple-element.99), kind=kOutput, calls=%fused_computation.9.clone.1 | convolution fusion | flops 536870912 | bytes 7341056 | tf_op jit(solution)/shard_map/while/body/eval_jaxpr/bjrk,bjkf->brf/dot_general | solution.py:73
  150.8 5.9 %gather_fusion = bf16[64,128,256]{2,1,0:T(8,128)(2,1)} fusion(bf16[113,128,256]{2,1,0:T(8,128)(2,1)} %get-tuple-element.101, s32[1024]{0:T(1024)S(1)} %pad_clamp_fusion.6), kind=kCustom, calls=%fused_computation.clone.1 | custom fusion | bytes 8388864 | tf_op jit(solution)/shard_map/while/body/eval_jaxpr/gather | solution.py:72
  156.7 4.6 %fusion.29 = f32[8,8,128,256]{3,2,1,0:T(8,128)} fusion(f32[8,8,128,256]{3,2,1,0:T(8,128)} %get-tuple-element.92, s32[]{:T(128)} %get-tuple-element.91, bf16[8,8,128,256]{3,2,1,0:T(8,128)(2,1)} %bitcast.66, bf16[8,8,8,128,128]{4,3,2,1,0:T(8,128)(2,1)} %get-tuple-element.99), kind=kOutput, calls=%fused_computation.9.clone.1 | convolution fusion | flops 536870912 | bytes 7341056 | tf_op jit(solution)/shard_map/while/body/eval_jaxpr/bjrk,bjkf->brf/dot_general | solution.py:73
  161.4 5.5 %fusion.12 = bf16[8192,256]{1,0:T(8,128)(2,1)S(1)} fusion(f32[8,8,128,256]{3,2,1,0:T(8,128)} %get-tuple-element.32, bf16[8192,256]{1,0:T(8,128)(2,1)} %param.17, pred[8192]{0:T(1024)(128)(4,1)S(1)} %iota_compare_fusion), kind=kLoop, calls=%fused_computation.17 | loop fusion | flops 8388608 | bytes 16785408 | tf_op jit(solution)/shard_map/convert_element_type | solution.py:84
  167.0 6.4 %multiply_reduce_fusion = (f32[256]{0:T(256)S(1)}, f32[256]{0:T(256)S(1)}, f32[8192,256]{1,0:T(8,128)}) fusion(pred[8192]{0:T(1024)(128)(4,1)S(1)} %iota_compare_fusion, bf16[8192,256]{1,0:T(8,128)(2,1)S(1)} %fusion.12, bf16[256,256]{1,0:T(8,128)(2,1)S(1)} %copy-done), kind=kOutput, calls=%fused_computation.19 | convolution fusion | flops 1082129920 | bytes 12724224 | tf_op jit(solution)/shard_map/dot_general | solution.py:87
  173.4 14.0 %all-reduce = (f32[256]{0:T(256)S(1)}, f32[1]{0:T(128)}, f32[256]{0:T(256)S(1)}) all-reduce(f32[256]{0:T(256)S(1)} %get-tuple-element.34, f32[1]{0:T(128)} %bitcast.20, f32[256]{0:T(256)S(1)} %get-tuple-element.33), channel_id=1, replica_groups=mesh['inner'=4,'outer'=8] {'outer'}, use_global_device_ids=true, to_apply=%region_3.4 | all-reduce | flops 513 | bytes 4104 | tf_op jit(solution)/shard_map/psum | solution.py:92
  187.4 12.2 %all-reduce.1 = (f32[256]{0:T(256)S(1)}, f32[]{:T(128)}, f32[256]{0:T(256)S(1)}) all-reduce(f32[256]{0:T(256)S(1)} %get-tuple-element.45, f32[]{:T(128)} %bitcast.21, f32[256]{0:T(256)S(1)} %get-tuple-element.47), channel_id=1, replica_groups=mesh['inner'=4,'outer'=8] {'inner'}, use_global_device_ids=true, to_apply=%region_4.5 | all-reduce | flops 513 | bytes 4104 | tf_op jit(solution)/shard_map/psum | solution.py:92
  200.3 6.1 %fusion.11 = bf16[8192,256]{1,0:T(8,128)(2,1)} fusion(bf16[256,256]{1,0:T(8,128)(2,1)S(1)} %copy-done.5, f32[8192,256]{1,0:T(8,128)} %get-tuple-element.53, f32[256]{0:T(256)S(1)} %copy-done.6, f32[256]{0:T(256)S(1)} %copy-done.7, f32[256]{0:T(256)S(1)} %get-tuple-element.51, f32[256]{0:T(256)S(1)} %get-tuple-element.52, f32[256]{0:T(256)S(1)} %copy-done.8, ...), kind=kOutput, calls=%fused_computation.15 | convolution fusion | flops 1092616192 | bytes 12727296 | tf_op jit(solution)/shard_map/dot_general | solution.py:98
  (71 shorter events, 5.7 us)
Async XLA Ops:
  0.0 166.9 %copy-start = (bf16[256,256]{1,0:T(8,128)(2,1)S(1)}, bf16[256,256]{1,0:T(8,128)(2,1)}, u32[]{:S(2)}) copy-start(bf16[256,256]{1,0:T(8,128)(2,1)} %param.27) | copy-start | bytes 393220
  2.8 15.4 %copy-start.3 = (s32[1,8,4]{1,2,0:T(4,128)S(1)}, s32[1,8,4]{1,2,0:T(4,128)}, u32[]{:S(2)}) copy-start(s32[1,8,4]{1,2,0:T(4,128)} %param.25) | copy-start | bytes 388
  2.8 15.6 %copy-start.1 = (s32[1,8]{1,0:T(1,128)S(1)}, s32[1,8]{1,0:T(1,128)}, u32[]{:S(2)}) copy-start(s32[1,8]{1,0:T(1,128)} %param.22) | copy-start | bytes 100
  9.0 13.4 %copy-start.9 = (s32[1,8]{1,0:T(1,128)S(1)}, s32[1,8]{1,0:T(1,128)}, u32[]{:S(2)}) copy-start(s32[1,8]{1,0:T(1,128)} %param.26) | copy-start | bytes 100
  12.9 27.8 %all-to-all-start = ((bf16[4,4,128,256]{3,2,1,0:T(8,128)(2,1)}), bf16[4,4,128,256]{3,2,1,0:T(8,128)(2,1)S(1)}, u32[]{:S(2)}, u32[]{:S(2)}) async-start(bf16[4,4,128,256]{3,2,1,0:T(8,128)(2,1)} %broadcast_select_fusion.2), calls=%async_computation | async-start | bytes 2097152 | tf_op jit(solution)/shard_map/all_to_all | solution.py:42
  18.4 26.5 %copy-start.2 = (s32[64,8]{0,1:T(8,128)S(1)}, s32[64,8]{0,1:T(8,128)}, u32[]{:S(2)}) copy-start(s32[64,8]{0,1:T(8,128)} %param.19) | copy-start | bytes 6148
  18.4 26.5 %copy-start.4 = (s32[64]{0:T(128)S(1)}, s32[64]{0:T(128)}, u32[]{:S(2)}) copy-start(s32[64]{0:T(128)} %param.20) | copy-start | bytes 772
  40.7 29.4 %all-to-all-start.1 = ((bf16[8,4,128,256]{3,2,1,0:T(8,128)(2,1)}), bf16[8,4,128,256]{3,2,1,0:T(8,128)(2,1)S(1)}, u32[]{:S(2)}, u32[]{:S(2)}) async-start(bf16[8,4,128,256]{3,2,1,0:T(8,128)(2,1)} %broadcast_select_fusion.1), calls=%async_computation.1 | async-start | bytes 4194304 | tf_op jit(solution)/shard_map/all_to_all | solution.py:49
  166.9 33.4 %copy-start.5 = (bf16[256,256]{1,0:T(8,128)(2,1)S(1)}, bf16[256,256]{1,0:T(8,128)(2,1)}, u32[]{:S(2)}) copy-start(bf16[256,256]{1,0:T(8,128)(2,1)} %param.30) | copy-start | bytes 393220
  167.0 33.4 %copy-start.6 = (f32[256]{0:T(256)S(1)}, f32[256]{0:T(256)}, u32[]{:S(2)}) copy-start(f32[256]{0:T(256)} %param.31) | copy-start | bytes 3076
  167.0 33.4 %copy-start.7 = (f32[256]{0:T(256)S(1)}, f32[256]{0:T(256)}, u32[]{:S(2)}) copy-start(f32[256]{0:T(256)} %param.29) | copy-start | bytes 3076
  167.0 33.4 %copy-start.8 = (f32[256]{0:T(256)S(1)}, f32[256]{0:T(256)}, u32[]{:S(2)}) copy-start(f32[256]{0:T(256)} %param.28) | copy-start | bytes 3076
